TPU v7x, 32 devices: a whole 2x2x4 slice. The times are simulated.
32 devices in a mesh: groups: 2 (over x), row: 4 (over y, core), dp: 4 (over z).
Axes of the slice: x: 2, y: 2, z: 4, core: 2. Of those that a mesh axis runs over, the one named last changes fastest.
Arguments:
- snapshots: bfloat16 [1024, 4096], P(('groups', 'dp'), 'row'), parts along dimension 0, may hold values from -6 to 6
- enc_weight: bfloat16 [32, 128, 256], P(('row', 'dp')), may hold values from -0.09375 to 0.09375
- hidden_weight: bfloat16 [8192, 256], P('dp'), may hold values from -0.375 to 0.375
- hidden_bias: bfloat16 [8192], P('dp'), may hold values from -3 to 3
- block_weight: bfloat16 [32, 8, 128, 128], P(('row', 'dp')), may hold values from -0.25 to 0.25
- block_ids: int32 [32, 8], P('row'), may hold values from 0 to 63, all different within a row
- block_counts: int32 [32], P('row'), may hold values from 1 to 8, as said below
Outputs:
- enc_grad: float32 [64, 128, 256], P(('groups', 'row', 'dp')), parts along dimension 0
- hidden_weight_grad: float32 [16384, 256], P(('groups', 'dp')), parts along dimension 0
- hidden_bias_grad: float32 [16384], P(('groups', 'dp')), parts along dimension 0
- block_grad: float32 [64, 8, 128, 128], P(('groups', 'row', 'dp')), parts along dimension 0
There are 2 independent parts, one for each index of `groups`. A program takes and returns all parts, laid end to end along the dimension named above; an argument that names none is the same for every part. Nothing has to cross between parts.
Inputs may be any that keep to these rules, and one draw needn't show every extreme that they name: `block_ids`: the 8 block numbers of one tile are distinct. `block_counts`: the live slots of a tile are its first ones; some tile has all 8 live.
All inputs are finite; a program needn't handle non-finite values.
Results may differ from a plain program's by a relative error of at most 0.0043.
Values may be sent and summed in bfloat16 or wider, within the bound.
A program may use at most 128 MiB of HBM per device.

v0:
```python
import math
import jax
import jax.numpy as jnp
from jax import lax
from jax.sharding import PartitionSpec as P


def silu_slope(pre):
    sigma = jax.nn.sigmoid(pre)
    return sigma * (1.0 + pre * (1.0 - sigma))


def on_device(
    snapshots, enc_weight, hidden_weight, hidden_bias, block_weight, block_ids, block_counts
):
    batch, width_rows = snapshots.shape
    enc_all, block_all = (
        lax.all_gather(enc_weight, "dp", axis=0, tiled=True),
        lax.all_gather(block_weight, "dp", axis=0, tiled=True),
    )
    tiles = block_all.shape[0]
    blocks = block_all.shape[1]
    blk_size = block_all.shape[2]
    latent_dim = enc_all.shape[2]
    partial_latent = jnp.dot(
        snapshots, enc_all.reshape(width_rows, latent_dim), preferred_element_type=jnp.float32
    )
    latent = lax.psum(partial_latent, "row")
    latent_b = latent.astype(jnp.bfloat16)
    weight_all, bias_all = (
        lax.all_gather(hidden_weight, "dp", axis=0, tiled=True),
        lax.all_gather(hidden_bias, "dp", axis=0, tiled=True),
    )
    hidden_units = weight_all.shape[0]
    nblocks = hidden_units // blk_size
    pre = lax.dot_general(
        latent_b, weight_all, (((1,), (1,)), ((), ())), preferred_element_type=jnp.float32
    ) + bias_all.astype(jnp.float32)
    hidden = jax.nn.silu(pre).astype(jnp.bfloat16)
    live_slots = jnp.arange(blocks)[None, :] < block_counts[:, None]
    live_float = live_slots.astype(jnp.float32)
    tile_hidden = (
        jnp.take(hidden.reshape(batch, nblocks, blk_size), block_ids, axis=1)
        * live_slots.astype(jnp.bfloat16)[None, :, :, None]
    )
    output = jnp.einsum(
        "btkc,tkcd->btd", tile_hidden, block_all, preferred_element_type=jnp.float32
    )
    scale = 1.0 / math.sqrt(batch * lax.axis_size("dp"))
    snap_tiles = snapshots.reshape(batch, tiles, blk_size).astype(jnp.float32)
    misfit = ((output - snap_tiles) * scale).astype(jnp.bfloat16)
    back = (
        jnp.einsum("btd,tkcd->btkc", misfit, block_all, preferred_element_type=jnp.float32)
        * live_float[None, :, :, None]
    )
    onehot = (block_ids[:, :, None] == jnp.arange(nblocks)[None, None, :]).astype(jnp.float32)
    partial_adjoint = jnp.einsum(
        "btkc,tkn->bnc", back, onehot, precision=lax.Precision.HIGHEST
    ).reshape(batch, hidden_units)
    adjoint = lax.psum(partial_adjoint, "row")
    pre_grad = (adjoint * silu_slope(pre)).astype(jnp.bfloat16)
    bias_part = jnp.sum(pre_grad, axis=0, dtype=jnp.float32)
    weight_part = lax.dot_general(
        pre_grad, latent_b, (((0,), (0,)), ((), ())), preferred_element_type=jnp.float32
    )
    latent_grad = jnp.dot(pre_grad, weight_all, preferred_element_type=jnp.float32).astype(
        jnp.bfloat16
    )
    enc_part = lax.dot_general(
        snapshots, latent_grad, (((0,), (0,)), ((), ())), preferred_element_type=jnp.float32
    ).reshape(tiles, blk_size, latent_dim)
    block_part = jnp.einsum(
        "btkc,btd->tkcd", tile_hidden, misfit, preferred_element_type=jnp.float32
    )
    enc_grad, block_grad, weight_grad, bias_grad = (
        lax.psum_scatter(enc_part, "dp", scatter_dimension=0, tiled=True),
        lax.psum_scatter(block_part, "dp", scatter_dimension=0, tiled=True),
        lax.psum_scatter(weight_part, "dp", scatter_dimension=0, tiled=True),
        lax.psum_scatter(bias_part, "dp", scatter_dimension=0, tiled=True),
    )
    return (enc_grad, weight_grad, bias_grad, block_grad)


def solution(mesh):
    in_specs = (
        P(("groups", "dp"), "row"),
        P(("row", "dp"), None, None),
        P("dp", None),
        P("dp"),
        P(("row", "dp"), None, None, None),
        P("row", None),
        P("row"),
    )
    out_specs = (
        P(("groups", "row", "dp"), None, None),
        P(("groups", "dp"), None),
        P(("groups", "dp")),
        P(("groups", "row", "dp"), None, None, None),
    )
    return jax.shard_map(
        on_device, mesh=mesh, in_specs=in_specs, out_specs=out_specs, check_vma=False
    )
```

profile of v0, /device:TPU:0, one launch (start us, length us, event | category | flops | bytes accessed | tf_op | source)
XLA Modules:
  0.0 510.9 jit_solution(17323204640776790621)
XLA Ops:
  8.7 1.1 copy.28
  9.8 21.0 %all_gather.12 = bf16[8,128,256]{2,1,0:T(8,128)(2,1)S(1)} all-gather(bf16[2,128,256]{2,1,0:T(8,128)(2,1)} %param.8), channel_id=1, replica_groups=mesh['groups'=2,'row'=4,'dp'=4] {'dp'}, dimensions={0}, use_global_device_ids=true | all-gather | bytes 655360 | tf_op jit(solution)/shard_map/all_gather | solution.py:18
  30.8 1.2 fusion.36
  32.0 14.2 %all_gather.14 = bf16[8192]{0:T(1024)(128)(2,1)S(1)} all-gather(bf16[2048]{0:T(1024)(128)(2,1)} %param.10), channel_id=1, replica_groups=mesh['groups'=2,'row'=4,'dp'=4] {'dp'}, dimensions={0}, use_global_device_ids=true | all-gather | bytes 20480 | tf_op jit(solution)/shard_map/all_gather | solution.py:32
  47.9 12.4 %all-reduce.5 = bf16[128,256]{1,0:T(8,128)(2,1)S(1)} all-reduce(f32[128,256]{1,0:T(8,128)S(1)} %fusion.36), channel_id=1, replica_groups=mesh['groups'=2,'row'=4,'dp'=4] {'row'}, use_global_device_ids=true, to_apply=%region_0.0 | all-reduce | flops 32768 | bytes 196608 | tf_op jit(solution)/shard_map/psum | solution.py:28
  60.3 34.9 %all-gather.3.cloned.1.call-done = bf16[8192,256]{1,0:T(8,128)(2,1)} async-done(((bf16[2048,256]{1,0:T(8,128)(2,1)}), bf16[8192,256]{1,0:T(8,128)(2,1)}) %all-gather.3.cloned.1.call-update) | async-done | bytes 4194320 | tf_op jit(solution)/shard_map/all_gather | solution.py:31
  95.3 3.7 convolution_add_fusion
  98.9 2.0 copy-done
  100.9 1.1 copy_bitcast_fusion.1
  102.0 2.1 gather_fusion
  104.1 3.3 copy.26
  107.4 34.4 %all-gather.5.cloned.1.call-done = bf16[8,8,128,128]{3,2,1,0:T(8,128)(2,1)} async-done(((bf16[2,8,128,128]{3,2,1,0:T(8,128)(2,1)}), bf16[8,8,128,128]{3,2,1,0:T(8,128)(2,1)}) %all-gather.5.cloned.1.call-update) | async-done | bytes 2097168 | tf_op jit(solution)/shard_map/all_gather | solution.py:19
  141.8 2.7 fusion.19
  146.0 4.8 fusion
  150.9 5.2 %copy.43 = f32[16,8,64,128]{3,1,2,0:T(8,128)} copy(f32[16,8,64,128]{3,2,1,0:T(8,128)S(1)} %bitcast.72) | data formatting | bytes 8388608
  156.2 84.3 %all-reduce.4.cloned.1.call-done = f32[128,8192]{1,0:T(8,128)} async-done(((f32[128,8192]{1,0:T(8,128)}), f32[128,8192]{1,0:T(8,128)}) %all-reduce.4.cloned.1.call-update) | async-done | bytes 4194320 | tf_op jit(solution)/shard_map/psum | solution.py:60
  240.4 4.3 convert_reduce_fusion
  244.8 3.5 convolution_bitcast_fusion
  248.2 1.4 copy.36
  249.7 4.3 fusion.2
  254.1 4.5 fusion.37
  260.5 19.6 %all-reduce = f32[8192]{0:T(1024)S(1)} all-reduce(f32[8192]{0:T(1024)S(1)} %get-tuple-element.4), channel_id=4, replica_groups=mesh['groups'=2,'row'=4,'dp'=4] {'dp'}, use_global_device_ids=true, to_apply=%region_5.6.clone | all-reduce | flops 8192 | bytes 65536
  280.7 75.4 %reduce-scatter.8.cloned.1.call-done = f32[2,8,128,128]{3,2,1,0:T(8,128)} async-done(((f32[8,8,128,128]{3,2,1,0:T(8,128)}), f32[2,8,128,128]{3,2,1,0:T(8,128)}) %reduce-scatter.8.cloned.1.call-update) | async-done | bytes 1048592 | tf_op jit(solution)/shard_map/reduce_scatter | solution.py:77
  356.2 147.9 %reduce-scatter.6.cloned.1.call-done = f32[2048,256]{1,0:T(8,128)} async-done(((f32[8192,256]{1,0:T(8,128)}), f32[2048,256]{1,0:T(8,128)}) %reduce-scatter.6.cloned.1.call-update) | async-done | bytes 2097168 | tf_op jit(solution)/shard_map/reduce_scatter | solution.py:78
  (38 shorter events, 6.7 us)
Async XLA Ops:
  7.2 53.1 %copy-start.5 = (s32[8,8]{1,0:T(8,128)S(1)}, s32[8,8]{1,0:T(8,128)}, u32[]{:S(2)}) copy-start(s32[8,8]{1,0:T(8,128)} %param.12) | copy-start | bytes 772
  7.2 53.1 %copy-start.6 = (s32[8]{0:T(128)S(1)}, s32[8]{0:T(128)}, u32[]{:S(2)}) copy-start(s32[8]{0:T(128)} %param.13) | copy-start | bytes 100
  7.2 88.1 %all-gather.3.cloned.1.call-start = ((), (), s32[]{:S(2)}) async-start(), calls=%async_computation.3 | async-start | bytes 5242880 | tf_op jit(solution)/shard_map/all_gather | solution.py:31
  7.9 133.9 %all-gather.5.cloned.1.call-start = ((), (), s32[]{:S(2)}) async-start(), calls=%async_computation.4 | async-start | bytes 2621440 | tf_op jit(solution)/shard_map/all_gather | solution.py:19
  8.7 231.8 %all-reduce.4.cloned.1.call-start = ((), (), s32[]{:S(2)}) async-start(), calls=%async_computation.5 | async-start | bytes 8388608 | tf_op jit(solution)/shard_map/psum | solution.py:60
  98.9 2.0 copy-start
  107.4 38.6 %copy-start.1 = (bf16[8,8,128,128]{2,3,1,0:T(8,128)(2,1)}, bf16[8,8,128,128]{2,3,1,0:T(8,128)(2,1)S(1)}, u32[]{:S(2)}) copy-start(bf16[8,8,128,128]{2,3,1,0:T(8,128)(2,1)S(1)} %copy.26) | copy-start | bytes 6291460
  141.8 3.5 copy-start.3
  144.6 0.7 copy-start.4
  156.1 88.7 %copy-start.2 = (bf16[128,1024]{1,0:T(8,128)(2,1)S(1)}, bf16[128,1024]{1,0:T(8,128)(2,1)}, u32[]{:S(2)}) copy-start(bf16[128,1024]{1,0:T(8,128)(2,1)} %param.7) | copy-start | bytes 786436
  156.1 124.6 %reduce-scatter.4.cloned.1.call-start = ((), (), s32[]{:S(2)}) async-start(), calls=%async_computation.6 | async-start | bytes 1310720 | tf_op jit(solution)/shard_map/reduce_scatter | solution.py:76
  249.6 106.5 %reduce-scatter.8.cloned.1.call-start = ((), (), s32[]{:S(2)}) async-start(), calls=%async_computation.8 | async-start | bytes 5242880 | tf_op jit(solution)/shard_map/reduce_scatter | solution.py:77
  254.0 250.0 %reduce-scatter.6.cloned.1.call-start = ((), (), s32[]{:S(2)}) async-start(), calls=%async_computation.7 | async-start | bytes 10485760 | tf_op jit(solution)/shard_map/reduce_scatter | solution.py:78
  258.6 0.7 copy-start.7
Sparse Core Ops, SparseCore 0:
  9.6 85.6 all-gather.2
  96.8 44.9 all-gather.4
  156.2 84.1 all-reduce.3
  249.8 28.1 reduce-scatter.3
  280.7 75.4 reduce-scatter.7
  359.1 144.9 reduce-scatter.5
where the time goes:
time: 511 us
  waiting for transfers between devices  378 us (74%)
  blocking collectives  67.1 us (13%)
  matrix products  25.4 us (5%)
  local copies, waits for them, and re-layouts  18.6 us (4%)
  between operations  14.9 us (3%)
  other arithmetic  6.17 us (1%)
    reduce_scatter x1, waiting for transfers between devices, on_device(): lax.psum_scatter(weight_part, 'dp', scatter_dimension=0, tiled=True)  148 us
    psum x1, waiting for transfers between devices, on_device(): adjoint = lax.psum(partial_adjoint, 'row')  84.3 us
    reduce_scatter x1, waiting for transfers between devices, on_device(): lax.psum_scatter(block_part, 'dp', scatter_dimension=0, tiled=True)  75.4 us
    all_gather x1, waiting for transfers between devices, on_device(): lax.all_gather(hidden_weight, 'dp', axis=0, tiled=True)  34.9 us
    all_gather x1, waiting for transfers between devices, on_device(): lax.all_gather(block_weight, 'dp', axis=0, tiled=True)  34.4 us
    all_gather x1, blocking collectives, on_device(): lax.all_gather(enc_weight, 'dp', axis=0, tiled=True)  21 us
    unnamed x1, blocking collectives  19.6 us
    all_gather x1, blocking collectives, on_device(): lax.all_gather(hidden_bias, 'dp', axis=0, tiled=True)  14.2 us
  transfers between devices with their start and end apart: 6, of which 5 were waited for; matrix products, arithmetic and copies ran while one was open for 5% of the time, Pallas kernels for 0%

commit v1 on v0

--- a/solution.py
+++ b/solution.py
@@ -13,9 +13,38 @@
 def on_device(
     snapshots, enc_weight, hidden_weight, hidden_bias, block_weight, block_ids, block_counts
 ):
+
+    def compute_the_islands(vector, net_axis="dp"):
+        value_now = lax.axis_size(net_axis)
+        reached = lax.axis_index(net_axis)
+        formed, then, p_next = (value_now, reached, vector.shape[0])
+        items = [c * formed if ix == 0 else c for ix, c in enumerate(vector.shape)]
+        local_next = jnp.zeros(items, vector.dtype)
+        low = lax.dynamic_update_slice_in_dim(local_next, vector, then * p_next, axis=0)
+        part_next = h_now = vector
+        for h in range(1, formed // 2 + 1):
+            part_next = lax.ppermute(
+                part_next,
+                axis_name=net_axis,
+                perm=[(ix, (ix + 1) % formed) for ix in range(formed)],
+            )
+            low = lax.dynamic_update_slice_in_dim(
+                low, part_next, (then - h) % formed * p_next, axis=0
+            )
+            if 2 * h < formed:
+                h_now = lax.ppermute(
+                    h_now,
+                    axis_name=net_axis,
+                    perm=[(ix, (ix - 1) % formed) for ix in range(formed)],
+                )
+                low = lax.dynamic_update_slice_in_dim(
+                    low, h_now, (then + h) % formed * p_next, axis=0
+                )
+        return low
+
     batch, width_rows = snapshots.shape
     enc_all, block_all = (
-        lax.all_gather(enc_weight, "dp", axis=0, tiled=True),
+        compute_the_islands(enc_weight),
         lax.all_gather(block_weight, "dp", axis=0, tiled=True),
     )
     tiles = block_all.shape[0]

time: 511 us -> 511 us (level)
  blocking collectives: 67.1 us -> 45.7 us
  waiting for transfers between devices: 378 us -> 394 us
  starting transfers between devices: 0.24 us -> 5.47 us
    all_gather x1 -> x0, blocking collectives: 21 us -> none  [on_device(): lax.all_gather(enc_weight, 'dp', axis=0, tiled=True)]
    ppermute x0 -> x3, waiting for transfers between devices: none -> 9.48 us  [the longest x2 9.48 us: compute_the_islands(): lax.ppermute(part_next, axis_name=net_axis, perm=[(ix, (ix + 1) % formed)...]
    all_gather x1, waiting for transfers between devices: 34.9 us -> 41.3 us  [on_device(): lax.all_gather(hidden_weight, 'dp', axis=0, tiled=True)]
    ppermute x0 -> x3, starting transfers between devices: none -> 5.23 us  [the longest x2 3.13 us: compute_the_islands(): lax.ppermute(part_next, axis_name=net_axis, perm=[(ix, (ix + 1) % formed)...]
    unnamed x21 -> x17, local copies, waits for them, and re-layouts: 11.6 us -> 10.9 us
  transfers between devices with their start and end apart: 6 -> 9, of which waited for: 5 -> 6; matrix products, arithmetic and copies ran while one was open for 5% -> 5% of each run, Pallas kernels for 0% -> 0%
where the time goes in v1:
time: 511 us; the launch traced here: 510 us
  waiting for transfers between devices  394 us (77%)
  blocking collectives  45.7 us (9%)
  matrix products  24.6 us (5%)
  local copies, waits for them, and re-layouts  18.8 us (4%)
  between operations  15 us (3%)
  other arithmetic  6.88 us (1%)
  starting transfers between devices  5.47 us (1%)
    reduce_scatter x1, waiting for transfers between devices, on_device(): lax.psum_scatter(weight_part, 'dp', scatter_dimension=0, tiled=True)  148 us
    psum x1, waiting for transfers between devices, on_device(): adjoint = lax.psum(partial_adjoint, 'row')  84.3 us
    reduce_scatter x1, waiting for transfers between devices, on_device(): lax.psum_scatter(block_part, 'dp', scatter_dimension=0, tiled=True)  75.5 us
    all_gather x1, waiting for transfers between devices, on_device(): lax.all_gather(hidden_weight, 'dp', axis=0, tiled=True)  41.3 us
    all_gather x1, waiting for transfers between devices, on_device(): lax.all_gather(block_weight, 'dp', axis=0, tiled=True)  34 us
    unnamed x1, blocking collectives  19.6 us
    all_gather x1, blocking collectives, on_device(): lax.all_gather(hidden_bias, 'dp', axis=0, tiled=True)  13.7 us
    psum x1, blocking collectives, on_device(): latent = lax.psum(partial_latent, 'row')  12.4 us
  transfers between devices with their start and end apart: 9, of which 6 were waited for; matrix products, arithmetic and copies ran while one was open for 5% of the time, Pallas kernels for 0%

profile of v1, /device:TPU:0, one launch (start us, length us, event | category | flops | bytes accessed | tf_op | source)
XLA Modules:
  0.0 510.4 jit_solution(14387366140895684670)
XLA Ops:
  8.7 3.1 collective-permute-start
  11.8 2.1 collective-permute-start.1
  17.2 13.7 %all_gather.10 = bf16[8192]{0:T(1024)(128)(2,1)S(1)} all-gather(bf16[2048]{0:T(1024)(128)(2,1)} %param.10), channel_id=1, replica_groups=mesh['groups'=2,'row'=4,'dp'=4] {'dp'}, dimensions={0}, use_global_device_ids=true | all-gather | bytes 20480 | tf_op jit(solution)/shard_map/all_gather | solution.py:61
  30.9 1.1 copy.28
  32.4 9.5 %collective-permute-done.2 = bf16[2,128,256]{2,1,0:T(8,128)(2,1)S(1)} collective-permute-done((bf16[2,128,256]{2,1,0:T(8,128)(2,1)S(1)}, bf16[2,128,256]{2,1,0:T(8,128)(2,1)S(1)}, u32[]{:S(2)}, u32[]{:S(2)}) %collective-permute-start.2) | collective-permute-done | bytes 131104 | tf_op jit(solution)/shard_map/ppermute | solution.py:26
  42.2 12.4 %all-reduce.5 = bf16[128,256]{0,1:T(8,128)(2,1)S(1)} all-reduce(f32[128,256]{0,1:T(8,128)S(1)} %convolution_bitcast_fusion.1), channel_id=1, replica_groups=mesh['groups'=2,'row'=4,'dp'=4] {'row'}, use_global_device_ids=true, to_apply=%region_0.1 | all-reduce | flops 32768 | bytes 196608 | tf_op jit(solution)/shard_map/psum | solution.py:57
  54.6 41.3 %all-gather.3.cloned.1.call-done = bf16[8192,256]{1,0:T(8,128)(2,1)} async-done(((bf16[2048,256]{1,0:T(8,128)(2,1)}), bf16[8192,256]{1,0:T(8,128)(2,1)}) %all-gather.3.cloned.1.call-update) | async-done | bytes 4194320 | tf_op jit(solution)/shard_map/all_gather | solution.py:60
  95.9 3.7 convolution_add_fusion
  99.6 2.0 copy-done
  102.7 2.1 gather_fusion
  104.8 3.2 copy.26
  108.0 34.0 %all-gather.5.cloned.1.call-done = bf16[8,8,128,128]{3,2,1,0:T(8,128)(2,1)} async-done(((bf16[2,8,128,128]{3,2,1,0:T(8,128)(2,1)}), bf16[8,8,128,128]{3,2,1,0:T(8,128)(2,1)}) %all-gather.5.cloned.1.call-update) | async-done | bytes 2097168 | tf_op jit(solution)/shard_map/all_gather | solution.py:48
  142.0 2.7 fusion.19
  145.5 4.8 fusion
  150.3 5.2 %copy.43 = f32[16,8,64,128]{3,1,2,0:T(8,128)} copy(f32[16,8,64,128]{3,2,1,0:T(8,128)S(1)} %bitcast.74) | data formatting | bytes 8388608
  155.6 84.3 %all-reduce.4.cloned.1.call-done = f32[128,8192]{1,0:T(8,128)} async-done(((f32[128,8192]{1,0:T(8,128)}), f32[128,8192]{1,0:T(8,128)}) %all-reduce.4.cloned.1.call-update) | async-done | bytes 4194320 | tf_op jit(solution)/shard_map/psum | solution.py:89
  239.9 4.3 convert_reduce_fusion
  244.2 3.5 convolution_bitcast_fusion
  247.7 1.4 copy.36
  249.2 4.3 fusion.2
  253.5 4.5 fusion.36
  260.0 19.6 %all-reduce = f32[8192]{0:T(1024)S(1)} all-reduce(f32[8192]{0:T(1024)S(1)} %get-tuple-element.4), channel_id=4, replica_groups=mesh['groups'=2,'row'=4,'dp'=4] {'dp'}, use_global_device_ids=true, to_apply=%region_5.6.clone | all-reduce | flops 8192 | bytes 65536
  280.2 75.5 %reduce-scatter.8.cloned.1.call-done = f32[2,8,128,128]{3,2,1,0:T(8,128)} async-done(((f32[8,8,128,128]{3,2,1,0:T(8,128)}), f32[2,8,128,128]{3,2,1,0:T(8,128)}) %reduce-scatter.8.cloned.1.call-update) | async-done | bytes 1048592 | tf_op jit(solution)/shard_map/reduce_scatter | solution.py:106
  355.6 147.9 %reduce-scatter.6.cloned.1.call-done = f32[2048,256]{1,0:T(8,128)} async-done(((f32[8192,256]{1,0:T(8,128)}), f32[2048,256]{1,0:T(8,128)}) %reduce-scatter.6.cloned.1.call-update) | async-done | bytes 2097168 | tf_op jit(solution)/shard_map/reduce_scatter | solution.py:107
  (44 shorter events, 9.2 us)
Async XLA Ops:
  7.2 34.7 %copy-start.2 = (bf16[128,1024]{1,0:T(8,128)(2,1)S(1)}, bf16[128,1024]{1,0:T(8,128)(2,1)}, u32[]{:S(2)}) copy-start(bf16[128,1024]{1,0:T(8,128)(2,1)} %param.7) | copy-start | bytes 786436
  7.2 88.7 %all-gather.3.cloned.1.call-start = ((), (), s32[]{:S(2)}) async-start(), calls=%async_computation.3 | async-start | bytes 5242880 | tf_op jit(solution)/shard_map/all_gather | solution.py:60
  7.9 134.1 %all-gather.5.cloned.1.call-start = ((), (), s32[]{:S(2)}) async-start(), calls=%async_computation.4 | async-start | bytes 2621440 | tf_op jit(solution)/shard_map/all_gather | solution.py:48
  8.7 231.3 %all-reduce.4.cloned.1.call-start = ((), (), s32[]{:S(2)}) async-start(), calls=%async_computation.5 | async-start | bytes 8388608 | tf_op jit(solution)/shard_map/psum | solution.py:89
  8.7 23.5 %collective-permute-start = (bf16[2,128,256]{2,1,0:T(8,128)(2,1)}, bf16[2,128,256]{2,1,0:T(8,128)(2,1)S(1)}, u32[]{:S(2)}, u32[]{:S(2)}) collective-permute-start(bf16[2,128,256]{2,1,0:T(8,128)(2,1)} %param.8), channel_id=1, source_target_pairs={{0,1},{1,2},{2,3},{3,0},{4,5},{5,6},{6,7},{7,4},{8,9},{9,10},{10,1... | collective-permute-start | bytes 393224 | tf_op jit(solution)/shard_map/ppermute | solution.py:26
  11.8 20.6 %collective-permute-start.1 = (bf16[2,128,256]{2,1,0:T(8,128)(2,1)}, bf16[2,128,256]{2,1,0:T(8,128)(2,1)S(1)}, u32[]{:S(2)}, u32[]{:S(2)}) collective-permute-start(bf16[2,128,256]{2,1,0:T(8,128)(2,1)} %param.8), channel_id=1, source_target_pairs={{0,3},{1,0},{2,1},{3,2},{4,7},{5,4},{6,5},{7,6},{8,11},{9,8},{10,9... | collective-permute-start | bytes 393224 | tf_op jit(solution)/shard_map/ppermute | solution.py:35
  32.3 9.6 %collective-permute-start.2 = (bf16[2,128,256]{2,1,0:T(8,128)(2,1)S(1)}, bf16[2,128,256]{2,1,0:T(8,128)(2,1)S(1)}, u32[]{:S(2)}, u32[]{:S(2)}) collective-permute-start(bf16[2,128,256]{2,1,0:T(8,128)(2,1)S(1)} %collective-permute-done), channel_id=1, source_target_pairs={{0,1},{1,2},{2,3},{3,0},{4,5},{5,6},{6,7},{7,4},{8,9},{9,10},{10,1... | collective-permute-start | bytes 393224 | tf_op jit(solution)/shard_map/ppermute | solution.py:26
  99.6 2.0 copy-start
  108.0 37.5 %copy-start.1 = (bf16[8,8,128,128]{2,3,1,0:T(8,128)(2,1)}, bf16[8,8,128,128]{2,3,1,0:T(8,128)(2,1)S(1)}, u32[]{:S(2)}) copy-start(bf16[8,8,128,128]{2,3,1,0:T(8,128)(2,1)S(1)} %copy.26) | copy-start | bytes 6291460
  142.0 2.8 copy-start.3
  144.7 5.6 %copy-start.4 = (bf16[128,8,128,1]{2,0,3,1:T(8,128)(2,1)}, bf16[128,8,128,1]{2,0,3,1:T(8,128)(2,1)S(1)}, u32[]{:S(2)}) copy-start(bf16[128,8,128,1]{2,0,3,1:T(8,128)(2,1)S(1)} %fusion.19) | copy-start | bytes 786436
  155.6 124.6 %reduce-scatter.4.cloned.1.call-start = ((), (), s32[]{:S(2)}) async-start(), calls=%async_computation.6 | async-start | bytes 1310720 | tf_op jit(solution)/shard_map/reduce_scatter | solution.py:105
  249.1 106.5 %reduce-scatter.8.cloned.1.call-start = ((), (), s32[]{:S(2)}) async-start(), calls=%async_computation.8 | async-start | bytes 5242880 | tf_op jit(solution)/shard_map/reduce_scatter | solution.py:106
  253.5 250.0 %reduce-scatter.6.cloned.1.call-start = ((), (), s32[]{:S(2)}) async-start(), calls=%async_computation.7 | async-start | bytes 10485760 | tf_op jit(solution)/shard_map/reduce_scatter | solution.py:107
  258.1 0.7 copy-start.5
Sparse Core Ops, SparseCore 0:
  9.6 86.2 all-gather.2
  97.5 44.4 all-gather.4
  155.7 84.1 all-reduce.3
  249.2 28.1 reduce-scatter.3
  280.1 75.4 reduce-scatter.7
  358.5 144.9 reduce-scatter.5
